TPU v7x, 1024 devices: a whole 4x4x32 slice. The times are simulated.
1024 devices in a mesh: prow: 16 (over y_hi, x, core), pcol: 64 (over y_lo, z).
Axes of the slice: x: 4, y: 4 (y_hi: 2, y_lo: 2; y = y_hi * 2 + y_lo), z: 32, core: 2. Of those that a mesh axis runs over, the one named last changes fastest.
Arguments:
- trailing: bfloat16 [8192, 65536], P('prow', 'pcol'), may hold values from -6 to 6
- lower_raw: bfloat16 [8192, 512], P(('prow', 'pcol')), may hold values from -0.25 to 0.25
- upper_raw: bfloat16 [512, 65536], P('prow', 'pcol'), may hold values from -6 to 6
- lower_inv: bfloat16 [512, 512], replicated, as said below
- upper_inv: bfloat16 [512, 512], replicated, as said below
Outputs:
- updated: bfloat16 [8192, 65536], P('prow', 'pcol')
Inputs may be any that keep to these rules, and one draw needn't show every extreme that they name: lower_inv is unit lower triangular. upper_inv is upper triangular with a positive diagonal.
All inputs are finite; a program needn't handle non-finite values.
Results may differ from a plain program's by a relative error of at most 0.0052.
Values may be sent and summed in bfloat16 or wider, within the bound.
No kernel may reach another device: no remote copies, remote signals or barrier semaphores. Data moves between devices by JAX's collectives and lax.ppermute only.
A program may use at most 32 MiB of HBM per device.

v0:
```python
import jax
import jax.numpy as jnp
from jax import lax
from jax.sharding import PartitionSpec as P


def on_device(trailing, lower_raw, upper_raw, lower_inv, upper_inv):
    upper_sum = jnp.dot(
        lower_inv,
        lax.all_gather(upper_raw, "prow", axis=0, tiled=True),
        preferred_element_type=jnp.float32,
    )
    upper_panel = upper_sum.astype(jnp.bfloat16)
    solved = jnp.dot(
        lax.all_gather(lower_raw, "pcol", axis=0, tiled=True),
        upper_inv,
        preferred_element_type=jnp.float32,
    ).astype(jnp.bfloat16)
    product = jnp.dot(solved, upper_panel, preferred_element_type=jnp.float32)
    return (trailing.astype(jnp.float32) - product).astype(jnp.bfloat16)


def solution(mesh):
    in_specs = (P("prow", "pcol"), P(("prow", "pcol"), None), P("prow", "pcol"), P(), P())
    out_specs = P("prow", "pcol")
    return jax.shard_map(
        on_device, mesh=mesh, in_specs=in_specs, out_specs=out_specs, check_vma=False
    )
```

profile of v0, /device:TPU:6, one launch (start us, length us, event | category | flops | bytes accessed | tf_op | source)
XLA Modules:
  0.0 157.2 jit_solution(7578423228907280846)
XLA Ops:
  6.5 0.0 copy-start
  6.5 0.0 all-gather.2.cloned.1.call-start
  6.5 0.7 all-gather.2.cloned.1.call-update
  7.3 136.9 %all_gather.6 = bf16[512,512]{1,0:T(8,128)(2,1)S(1)} all-gather(bf16[8,512]{1,0:T(8,128)(2,1)} %param.6), channel_id=1, replica_groups=mesh['prow'=16,'pcol'=64] {'pcol'}, dimensions={0}, use_global_device_ids=true | all-gather | bytes 532480 | tf_op jit(solution)/shard_map/all_gather | solution.py:15
  144.1 0.0 copy-start.1
  144.1 0.0 copy-start.2
  144.1 0.0 all-gather.2.cloned.1.call-done
  144.1 0.0 copy-done
  144.1 3.1 %convolution_convert_fusion = bf16[512,1024]{1,0:T(8,128)(2,1)} fusion(bf16[512,512]{1,0:T(8,128)(2,1)S(1)} %copy-done, bf16[512,1024]{1,0:T(8,128)(2,1)} %all-gather.2.cloned.1.call-done), kind=kOutput, calls=%fused_computation.1 | convolution fusion | flops 537395200 | bytes 2621440 | tf_op jit(solution)/shard_map/dot_general | solution.py:8
  147.2 0.0 copy-done.1
  147.2 0.0 copy-done.2
  147.2 3.2 %subtract_convert_fusion = bf16[512,1024]{1,0:T(8,128)(2,1)} fusion(bf16[512,1024]{1,0:T(8,128)(2,1)S(1)} %copy-done.1, bf16[512,1024]{1,0:T(8,128)(2,1)} %convolution_convert_fusion, bf16[512,512]{1,0:T(8,128)(2,1)S(1)} %all_gather.6, bf16[512,512]{1,0:T(8,128)(2,1)S(1)} %copy-done.2), kind=kOutput, calls=%fused_computation | convolution fusion | flops 807141376 | bytes 4194304 | tf_op jit(solution)/shard_map/dot_general | solution.py:19
Async XLA Ops:
  6.5 137.6 %copy-start = (bf16[512,512]{1,0:T(8,128)(2,1)S(1)}, bf16[512,512]{1,0:T(8,128)(2,1)}, u32[]{:S(2)}) copy-start(bf16[512,512]{1,0:T(8,128)(2,1)} %param.8) | copy-start | bytes 1572868
  6.5 137.6 %all-gather.2.cloned.1.call-start = ((), (), s32[]{:S(2)}) async-start(), calls=%async_computation | async-start | bytes 1114112 | tf_op jit(solution)/shard_map/all_gather | solution.py:10
  144.1 3.1 %copy-start.1 = (bf16[512,1024]{1,0:T(8,128)(2,1)S(1)}, bf16[512,1024]{1,0:T(8,128)(2,1)}, u32[]{:S(2)}) copy-start(bf16[512,1024]{1,0:T(8,128)(2,1)} %param.5) | copy-start | bytes 3145732
  144.1 3.1 %copy-start.2 = (bf16[512,512]{1,0:T(8,128)(2,1)S(1)}, bf16[512,512]{1,0:T(8,128)(2,1)}, u32[]{:S(2)}) copy-start(bf16[512,512]{1,0:T(8,128)(2,1)} %param.9) | copy-start | bytes 1572868
Sparse Core Ops, SparseCore 0:
  11.8 88.3 all-gather.1
where the time goes:
time: 157 us
  blocking collectives  137 us (87%)
  between operations  13.4 us (9%)
  matrix products  6.26 us (4%)
    all_gather x1, blocking collectives, on_device(): lax.all_gather(lower_raw, 'pcol', axis=0, tiled=True)  137 us
    dot_general x1, matrix products, on_device(): product = jnp.dot(solved, upper_panel, preferred_element_type=jnp.float32)  3.18 us
  transfers between devices with their start and end apart: 1, of which 0 were waited for; matrix products, arithmetic and copies ran while one was open for 0% of the time, Pallas kernels for 0%

commit v1 on v0

v1 whole, which is shorter than its diff:
```python
import jax
import jax.numpy as jnp
from jax import lax
from jax.sharding import Mesh, PartitionSpec as P

AXES = ("y_hi", "x", "core", "y_lo", "z_far", "z_near")
SIZES = (2, 4, 2, 2, 16, 2)
FAR, NEAR = SIZES[4], SIZES[5]


def share(block, axes, count):
    copies = jnp.broadcast_to(block[None], (count,) + block.shape)
    return lax.all_to_all(copies, axes, 0, 0)


def on_device(trailing, lower_raw, upper_raw, lower_inv, upper_inv):
    far = share(lower_raw, "z_far", FAR)
    core = lax.axis_index("core")
    upper = lax.all_gather(upper_raw, "y_hi", axis=0)
    upper = lax.all_gather(upper, "x", axis=0).reshape(256, 1024)
    far, upper = lax.optimization_barrier((far, upper))
    near = share(far.reshape(FAR * 8, 512), ("y_lo", "z_near"), 2 * NEAR)
    other = lax.ppermute(upper, "core", [(0, 1), (1, 0)])
    inverse = lower_inv.reshape(512, 2, 4, 2, 32)
    inverse = inverse.transpose(3, 0, 2, 1, 4).reshape(2, 512, 256)
    mine = lax.dynamic_index_in_dim(inverse, core, 0, keepdims=False)
    theirs = lax.dynamic_index_in_dim(inverse, 1 - core, 0, keepdims=False)
    upper_panel = (
        jnp.dot(mine, upper, preferred_element_type=jnp.float32)
        + jnp.dot(theirs, other, preferred_element_type=jnp.float32)
    ).astype(jnp.bfloat16)
    lower = jnp.swapaxes(near.reshape(2, NEAR, FAR, 8, 512), 1, 2).reshape(512, 512)
    solved = jnp.dot(lower, upper_inv, preferred_element_type=jnp.float32).astype(jnp.bfloat16)
    product = jnp.dot(solved, upper_panel, preferred_element_type=jnp.float32)
    return (trailing.astype(jnp.float32) - product).astype(jnp.bfloat16)


def solution(mesh):
    mesh = Mesh(mesh.devices.reshape(SIZES), AXES)
    rows, columns = AXES[:3], AXES[3:]
    in_specs = (P(rows, columns), P(AXES, None), P(rows, columns), P(), P())
    return jax.shard_map(
        on_device, mesh=mesh, in_specs=in_specs, out_specs=P(rows, columns), check_vma=False
    )
```

time: 157 us -> 74.5 us (0.47)
  blocking collectives: 137 us -> 19.5 us
  starting transfers between devices: 0.01 us -> 34.5 us
  between operations: 13.4 us -> 0.07 us
  waiting for transfers between devices: 0.71 us -> 8.61 us
  local copies, waits for them, and re-layouts: 0.01 us -> 4.43 us
    all_gather x1 -> x2, blocking collectives: 137 us -> 19.5 us  [the longest x1 12.9 us: on_device(): upper = lax.all_gather(upper, 'x', axis=0).reshape(256, 1024)]
    all_to_all x0 -> x2, starting transfers between devices: none -> 32.6 us  [share(): return lax.all_to_all(copies, axes, 0, 0)]
    all_to_all x0 -> x2, waiting for transfers between devices: none -> 8.61 us  [share(): return lax.all_to_all(copies, axes, 0, 0)]
    broadcast_in_dim x0 -> x2, local copies, waits for them, and re-layouts: none -> 2.28 us  [share(): copies = jnp.broadcast_to(block[None], (count,) + block.shape)]
    transpose x0 -> x2, local copies, waits for them, and re-layouts: none -> 1.93 us  [the longest x1 1.09 us: on_device(): jnp.swapaxes(near.reshape(2, NEAR, FAR, 8, 512), 1, 2).reshape(512, 512)]
    ppermute x0 -> x1, starting transfers between devices: none -> 1.91 us  [on_device(): other = lax.ppermute(upper, 'core', [(0, 1), (1, 0)])]
  transfers between devices with their start and end apart: 1 -> 3, of which waited for: 0 -> 2; matrix products, arithmetic and copies ran while one was open for 0% -> 7% of each run, Pallas kernels for 0% -> 0%
where the time goes in v1:
time: 74.5 us; the launch traced here: 73.4 us
  starting transfers between devices  34.5 us (46%)
  blocking collectives  19.5 us (26%)
  waiting for transfers between devices  8.61 us (12%)
  matrix products  6.27 us (8%)
  local copies, waits for them, and re-layouts  4.43 us (6%)
    all_to_all x2, starting transfers between devices, share(): return lax.all_to_all(copies, axes, 0, 0)  32.6 us
    all_gather x1, blocking collectives, on_device(): upper = lax.all_gather(upper, 'x', axis=0).reshape(256, 1024)  12.9 us
    all_to_all x2, waiting for transfers between devices, share(): return lax.all_to_all(copies, axes, 0, 0)  8.61 us
    all_gather x1, blocking collectives, on_device(): upper = lax.all_gather(upper_raw, 'y_hi', axis=0)  6.66 us
    dot_general x1, matrix products, on_device(): product = jnp.dot(solved, upper_panel, preferred_element_type=jnp.float32)  3.61 us
    broadcast_in_dim x2, local copies, waits for them, and re-layouts, share(): copies = jnp.broadcast_to(block[None], (count,) + block.shape)  2.28 us
    ppermute x1, starting transfers between devices, on_device(): other = lax.ppermute(upper, 'core', [(0, 1), (1, 0)])  1.91 us
  transfers between devices with their start and end apart: 3, of which 2 were waited for; matrix products, arithmetic and copies ran while one was open for 7% of the time, Pallas kernels for 0%

profile of v1, /device:TPU:6, one launch (start us, length us, event | category | flops | bytes accessed | tf_op | source)
XLA Modules:
  0.0 73.4 jit_solution(1968035994639179677)
XLA Ops:
  0.0 0.0 copy-start
  0.0 0.0 copy-start.1
  0.0 1.4 %broadcast_in_dim.6 = bf16[16,8,512]{2,1,0:T(8,128)(2,1)} broadcast(bf16[8,512]{1,0:T(8,128)(2,1)} %param.6), dimensions={1,2} | broadcast | bytes 139264 | tf_op jit(solution)/shard_map/broadcast_in_dim | solution.py:12
  1.5 28.4 %all-to-all-start = ((bf16[16,8,512]{2,1,0:T(8,128)(2,1)}), bf16[16,8,512]{2,1,0:T(8,128)(2,1)S(1)}, u32[]{:S(2)}, u32[]{:S(2)}) async-start(bf16[16,8,512]{2,1,0:T(8,128)(2,1)} %broadcast_in_dim.6), calls=%async_computation | async-start | bytes 262144 | tf_op jit(solution)/shard_map/all_to_all | solution.py:13
  29.9 6.7 %all-gather = bf16[64,1024]{1,0:T(8,128)(2,1)S(1)} all-gather(bf16[32,1024]{1,0:T(8,128)(2,1)} %param.7), channel_id=2, replica_groups=mesh['y_hi'=2,'x'=4,'core'=2,'y_lo'=2,'z_far'=16,'z_near'=2] {'y_hi'}, dimensions={0}, use_global_device_ids=true | all-gather | bytes 196608 | tf_op jit(solution)/shard_map/all_gather | solution.py:19
  36.6 12.9 %all-gather.1 = bf16[8,32,1024]{2,1,0:T(8,128)(2,1)S(1)} all-gather(bf16[2,32,1024]{2,1,0:T(8,128)(2,1)S(1)} %bitcast.30), channel_id=3, replica_groups=mesh['y_hi'=2,'x'=4,'core'=2,'y_lo'=2,'z_far'=16,'z_near'=2] {'x'}, dimensions={0}, use_global_device_ids=true | all-gather | bytes 655360 | tf_op jit(solution)/shard_map/all_gather | solution.py:20
  49.4 6.4 %all-to-all-done = bf16[16,8,512]{2,1,0:T(8,128)(2,1)S(1)} async-done(((bf16[16,8,512]{2,1,0:T(8,128)(2,1)}), bf16[16,8,512]{2,1,0:T(8,128)(2,1)S(1)}, u32[]{:S(2)}, u32[]{:S(2)}) %all-to-all-start) | async-done | bytes 131104 | tf_op jit(solution)/shard_map/all_to_all | solution.py:13
  55.8 0.8 %broadcast_in_dim.15 = bf16[4,128,512]{2,1,0:T(8,128)(2,1)} broadcast(bf16[128,512]{1,0:T(8,128)(2,1)S(1)} %bitcast.29), dimensions={1,2} | broadcast | bytes 655360 | tf_op jit(solution)/shard_map/broadcast_in_dim | solution.py:12
  56.7 4.1 %all-to-all-start.1 = ((bf16[4,128,512]{2,1,0:T(8,128)(2,1)}), bf16[4,128,512]{2,1,0:T(8,128)(2,1)}, u32[]{:S(2)}, u32[]{:S(2)}) async-start(bf16[4,128,512]{2,1,0:T(8,128)(2,1)} %broadcast_in_dim.15), calls=%async_computation.1 | async-start | bytes 1048576 | tf_op jit(solution)/shard_map/all_to_all | solution.py:13
  60.8 0.0 copy-done.1
  60.8 0.2 copy.12
  61.0 0.8 %copy.13 = bf16[2,512,4,2,32]{1,4,3,2,0:T(8,128)(2,1)} copy(bf16[2,512,4,2,32]{1,4,0,2,3:T(8,128)(2,1)S(1)} %bitcast.26) | data formatting | bytes 1048576 | tf_op jit(solution)/shard_map/transpose | solution.py:25
  61.9 1.9 %collective-permute-start = (bf16[256,1024]{1,0:T(8,128)(2,1)S(1)}, bf16[256,1024]{1,0:T(8,128)(2,1)}, u32[]{:S(2)}, u32[]{:S(2)}) collective-permute-start(bf16[256,1024]{1,0:T(8,128)(2,1)S(1)} %bitcast.24), channel_id=1, source_target_pairs={{0,64},{64,0},{1,65},{65,1},{2,66},{66,2},{3,67},{67,3},{4,68},{68... | collective-permute-start | bytes 1572872 | tf_op jit(solution)/shard_map/ppermute | solution.py:23
  63.8 1.4 %fusion.2 = f32[512,1024]{1,0:T(8,128)S(1)} fusion(bf16[256,1024]{1,0:T(8,128)(2,1)S(1)} %bitcast.25, bf16[2,512,256]{1,2,0:T(8,128)(2,1)} %bitcast.27, s32[]{:T(128)S(6)} %select_n.7), kind=kOutput, calls=%fused_computation.4 | convolution fusion | flops 268435456 | bytes 2883588 | tf_op jit(solution)/shard_map/dot_general | solution.py:29
  65.2 2.2 %all-to-all-done.1 = bf16[4,128,512]{2,1,0:T(8,128)(2,1)} async-done(((bf16[4,128,512]{2,1,0:T(8,128)(2,1)}), bf16[4,128,512]{2,1,0:T(8,128)(2,1)}, u32[]{:S(2)}, u32[]{:S(2)}) %all-to-all-start.1) | async-done | bytes 524320 | tf_op jit(solution)/shard_map/all_to_all | solution.py:13
  67.4 1.1 %copy.11 = bf16[2,16,2,8,512]{4,3,2,1,0:T(8,128)(2,1)S(1)} copy(bf16[2,16,2,8,512]{4,3,1,2,0:T(8,128)(2,1)} %bitcast.4) | data formatting | bytes 1048576 | tf_op jit(solution)/shard_map/transpose | solution.py:32
  68.5 0.0 copy-done
  68.6 1.2 %convolution_convert_fusion = bf16[512,512]{1,0:T(8,128)(2,1)} fusion(bf16[512,512]{1,0:T(8,128)(2,1)S(1)} %bitcast.23, bf16[512,512]{1,0:T(8,128)(2,1)S(1)} %copy-done), kind=kOutput, calls=%fused_computation.2 | convolution fusion | flops 268697600 | bytes 1572864 | tf_op jit(solution)/shard_map/dot_general | solution.py:33
  69.8 0.0 collective-permute-done
  69.8 3.6 %subtract_convert_fusion = bf16[512,1024]{1,0:T(8,128)(2,1)} fusion(bf16[512,1024]{1,0:T(8,128)(2,1)} %param.5, bf16[512,512]{1,0:T(8,128)(2,1)} %convolution_convert_fusion, f32[512,1024]{1,0:T(8,128)S(1)} %fusion.2, bf16[256,1024]{1,0:T(8,128)(2,1)} %collective-permute-done, bf16[2,512,256]{1,2,0:T(8,128)(2,1)} %bitcast.28, s32[]{:T(128)S(6)} %select_n.8), kind=kOutput, calls=%fused_computation | convolution fusion | flops 807927808 | bytes 5505028 | tf_op jit(solution)/shard_map/dot_general | solution.py:34
Async XLA Ops:
  0.0 68.5 %copy-start = (bf16[512,512]{1,0:T(8,128)(2,1)S(1)}, bf16[512,512]{1,0:T(8,128)(2,1)}, u32[]{:S(2)}) copy-start(bf16[512,512]{1,0:T(8,128)(2,1)} %param.9) | copy-start | bytes 1572868
  0.0 60.8 %copy-start.1 = (bf16[512,512]{1,0:T(8,128)(2,1)S(1)}, bf16[512,512]{1,0:T(8,128)(2,1)}, u32[]{:S(2)}) copy-start(bf16[512,512]{1,0:T(8,128)(2,1)} %param.8) | copy-start | bytes 1572868
  1.5 54.4 %all-to-all-start = ((bf16[16,8,512]{2,1,0:T(8,128)(2,1)}), bf16[16,8,512]{2,1,0:T(8,128)(2,1)S(1)}, u32[]{:S(2)}, u32[]{:S(2)}) async-start(bf16[16,8,512]{2,1,0:T(8,128)(2,1)} %broadcast_in_dim.6), calls=%async_computation | async-start | bytes 262144 | tf_op jit(solution)/shard_map/all_to_all | solution.py:13
  56.7 10.8 %all-to-all-start.1 = ((bf16[4,128,512]{2,1,0:T(8,128)(2,1)}), bf16[4,128,512]{2,1,0:T(8,128)(2,1)}, u32[]{:S(2)}, u32[]{:S(2)}) async-start(bf16[4,128,512]{2,1,0:T(8,128)(2,1)} %broadcast_in_dim.15), calls=%async_computation.1 | async-start | bytes 1048576 | tf_op jit(solution)/shard_map/all_to_all | solution.py:13
  61.9 7.9 %collective-permute-start = (bf16[256,1024]{1,0:T(8,128)(2,1)S(1)}, bf16[256,1024]{1,0:T(8,128)(2,1)}, u32[]{:S(2)}, u32[]{:S(2)}) collective-permute-start(bf16[256,1024]{1,0:T(8,128)(2,1)S(1)} %bitcast.24), channel_id=1, source_target_pairs={{0,64},{64,0},{1,65},{65,1},{2,66},{66,2},{3,67},{67,3},{4,68},{68... | collective-permute-start | bytes 1572872 | tf_op jit(solution)/shard_map/ppermute | solution.py:23

commit v2 on v1

v2 whole, which is shorter than its diff:
```python
import functools

import jax
import jax.numpy as jnp
from jax import lax
from jax.experimental import pallas as pl
from jax.experimental.pallas import tpu as pltpu
from jax.sharding import Mesh, PartitionSpec as P

AXES = ("y_hi", "x", "core", "y_lo", "z")
SIZES = (2, 4, 2, 2, 32)
NEAR = 2
FAR = 32 // NEAR
FIRST = 24
ORDER = [(FIRST + NEAR * i) % 32 // NEAR for i in range(FAR)]
GROUPS = [[NEAR * i + j for i in ORDER] for j in range(NEAR)]
SWAP = [(0, 1), (1, 0)]
ROWS = FAR * 8


def gather_far(block):
    copies = jnp.broadcast_to(block[None], (FAR,) + block.shape)
    return lax.all_to_all(copies, "z", 0, 0, axis_index_groups=GROUPS)


def gather_near(block):
    copies = jnp.broadcast_to(block[None], (2 * NEAR,) + block.shape)
    groups = [
        [32 * y + NEAR * i + j for y in range(2) for j in range(NEAR)] for i in range(FAR)
    ]
    return lax.all_to_all(copies, ("y_lo", "z"), 0, 0, axis_index_groups=groups)


def update(parts_ref, inverse_ref, upper_ref, trailing_ref, out_ref, solved, done, sems):
    for part in range(2 * NEAR):
        rows = jnp.dot(parts_ref[part], inverse_ref[...], preferred_element_type=jnp.float32)
        for i, place in enumerate(ORDER):
            at = 8 * (32 * (part // NEAR) + NEAR * place + part % NEAR)
            solved[pl.ds(at, 8), :] = rows[i * 8 : i * 8 + 8]
    copies = []
    for step in range(4):
        rows = pl.ds(step * 128, 128)
        product = jnp.dot(
            solved[rows, :].astype(jnp.bfloat16), upper_ref[...], preferred_element_type=jnp.float32
        )
        done[rows, :] = (trailing_ref[rows, :].astype(jnp.float32) - product).astype(jnp.bfloat16)
        copies.append(pltpu.make_async_copy(done.at[rows, :], out_ref.at[rows, :], sems.at[step]))
        copies[-1].start()
    for copy in copies:
        copy.wait()


def on_device(trailing, lower_raw, upper_raw, lower_inv, upper_inv):
    core = lax.axis_index("core")
    y_hi = lax.axis_index("y_hi")
    far = gather_far(lower_raw)
    upper = lax.all_gather(upper_raw, "y_hi", axis=0)
    upper = lax.all_gather(upper, "x", axis=0).reshape(256, 1024)
    far, upper = lax.optimization_barrier((far, upper))
    parts = gather_near(far.reshape(ROWS, 512))
    other = lax.ppermute(upper, "core", SWAP)
    inverse = lower_inv.reshape(512, 2, 4, 2, 32)
    inverse = inverse.transpose(3, 0, 2, 1, 4).reshape(2, 512, 256)
    mine = lax.dynamic_index_in_dim(inverse, core, 0, keepdims=False)
    theirs = lax.dynamic_index_in_dim(inverse, 1 - core, 0, keepdims=False)
    upper_panel = (
        jnp.dot(mine, upper, preferred_element_type=jnp.float32)
        + jnp.dot(theirs, other, preferred_element_type=jnp.float32)
    ).astype(jnp.bfloat16)
    whole = pl.BlockSpec(memory_space=pltpu.VMEM)
    return pl.pallas_call(
        update,
        out_shape=jax.ShapeDtypeStruct((512, 1024), jnp.bfloat16),
        in_specs=[whole, whole, whole, whole],
        out_specs=pl.BlockSpec(memory_space=pl.ANY),
        scratch_shapes=[
            pltpu.VMEM((512, 512), jnp.float32),
            pltpu.VMEM((512, 1024), jnp.bfloat16),
            pltpu.SemaphoreType.DMA((4,)),
        ],
        compiler_params=pltpu.CompilerParams(vmem_limit_bytes=24 * 2**20),
        cost_estimate=pl.CostEstimate(
            flops=2 * 512 * 512 * 1536, bytes_accessed=4 * 2**20, transcendentals=0
        ),
        name="update",
    )(parts, upper_inv, upper_panel, trailing)


def solution(mesh):
    mesh = Mesh(mesh.devices.reshape(SIZES), AXES)
    rows, columns = AXES[:3], AXES[3:]
    in_specs = (P(rows, columns), P(AXES, None), P(rows, columns), P(), P())
    return jax.shard_map(
        on_device, mesh=mesh, in_specs=in_specs, out_specs=P(rows, columns), check_vma=False
    )
```

time: 74.5 us -> 64.9 us (0.87)
  waiting for transfers between devices: 8.61 us -> 3.29 us
  matrix products: 6.27 us -> 2.07 us
  Pallas kernels: 0 us -> 1.74 us
  local copies, waits for them, and re-layouts: 4.43 us -> 3.31 us
    all_to_all x2, waiting for transfers between devices: 8.61 us -> 2.85 us  [the longest x1 1.86 us: gather_far(): return lax.all_to_all(copies, 'z', 0, 0, axis_index_groups=GROUPS)]
    dot_general x2 -> x1, matrix products: 4.85 us -> 1.61 us  [on_device(): jnp.dot(theirs, other, preferred_element_type=jnp.float32)]
    pallas_call x0 -> x1, Pallas kernels: none -> 1.74 us  [on_device(): pl.pallas_call(update, out_shape=jax.ShapeDtypeStruct((512, 1024), jnp.bf...]
    transpose x1 -> x0, local copies, waits for them, and re-layouts: 1.09 us -> none  [on_device(): jnp.swapaxes(near.reshape(2, NEAR, FAR, 8, 512), 1, 2).reshape(512, 512)]
    dot_general x1, matrix products: 1.41 us -> 0.46 us  [on_device(): jnp.dot(mine, upper, preferred_element_type=jnp.float32)]
    unnamed x5 -> x9, local copies, waits for them, and re-layouts: 0.22 us -> 1.02 us
    transpose x1, local copies, waits for them, and re-layouts: 0.84 us -> 0.04 us  [on_device(): inverse = inverse.transpose(3, 0, 2, 1, 4).reshape(2, 512, 256)]
  transfers between devices with their start and end apart: 3 -> 3, of which waited for: 2 -> 3; matrix products, arithmetic and copies ran while one was open for 7% -> 4% of each run, Pallas kernels for 0% -> 0%
where the time goes in v2:
time: 64.9 us; the launch traced here: 64.3 us
  starting transfers between devices  34.3 us (53%)
  blocking collectives  19.5 us (30%)
  local copies, waits for them, and re-layouts  3.31 us (5%)
  waiting for transfers between devices  3.29 us (5%)
  matrix products  2.07 us (3%)
  Pallas kernels  1.74 us (3%)
    all_to_all x1, starting transfers between devices, gather_far(): return lax.all_to_all(copies, 'z', 0, 0, axis_index_groups=GROUPS)  28.9 us
    all_gather x1, blocking collectives, on_device(): upper = lax.all_gather(upper, 'x', axis=0).reshape(256, 1024)  12.9 us
    all_gather x1, blocking collectives, on_device(): upper = lax.all_gather(upper_raw, 'y_hi', axis=0)  6.65 us
    all_to_all x1, starting transfers between devices, gather_near(): return lax.all_to_all(copies, ('y_lo', 'z'), 0, 0, axis_index_groups=groups)  3.47 us
    ppermute x1, starting transfers between devices, on_device(): other = lax.ppermute(upper, 'core', SWAP)  1.92 us
    all_to_all x1, waiting for transfers between devices, gather_far(): return lax.all_to_all(copies, 'z', 0, 0, axis_index_groups=GROUPS)  1.86 us
    pallas_call x1, Pallas kernels, on_device(): pl.pallas_call(update, out_shape=jax.ShapeDtypeStruct((512, 1024), jnp.bf...  1.74 us
    dot_general x1, matrix products, on_device(): jnp.dot(theirs, other, preferred_element_type=jnp.float32)  1.61 us
  transfers between devices with their start and end apart: 3, of which 3 were waited for; matrix products, arithmetic and copies ran while one was open for 4% of the time, Pallas kernels for 0%

profile of v2, /device:TPU:6, one launch (start us, length us, event | category | flops | bytes accessed | tf_op | source)
XLA Modules:
  0.0 64.3 jit_solution(4158360088934779559)
XLA Ops:
  0.0 0.0 copy-start.3
  0.0 1.4 %broadcast_in_dim.6 = bf16[16,8,512]{2,1,0:T(8,128)(2,1)} broadcast(bf16[8,512]{1,0:T(8,128)(2,1)} %param.6), dimensions={1,2} | broadcast | bytes 139264 | tf_op jit(solution)/shard_map/broadcast_in_dim | solution.py:22
  1.4 28.9 %all-to-all-start = ((bf16[16,8,512]{2,1,0:T(8,128)(2,1)}), bf16[16,8,512]{2,1,0:T(8,128)(2,1)S(1)}, u32[]{:S(2)}, u32[]{:S(2)}) async-start(bf16[16,8,512]{2,1,0:T(8,128)(2,1)} %broadcast_in_dim.6), calls=%async_computation | async-start | bytes 262144 | tf_op jit(solution)/shard_map/all_to_all | solution.py:23
  30.3 6.6 %all-gather = bf16[64,1024]{1,0:T(8,128)(2,1)S(1)} all-gather(bf16[32,1024]{1,0:T(8,128)(2,1)} %param.7), channel_id=2, replica_groups=mesh['y_hi'=2,'x'=4,'core'=2,'y_lo'=2,'z'=32] {'y_hi'}, dimensions={0}, use_global_device_ids=true | all-gather | bytes 196608 | tf_op jit(solution)/shard_map/all_gather | solution.py:57
  37.0 12.9 %all-gather.1 = bf16[8,32,1024]{2,1,0:T(8,128)(2,1)S(1)} all-gather(bf16[2,32,1024]{2,1,0:T(8,128)(2,1)S(1)} %bitcast.21), channel_id=3, replica_groups=mesh['y_hi'=2,'x'=4,'core'=2,'y_lo'=2,'z'=32] {'x'}, dimensions={0}, use_global_device_ids=true | all-gather | bytes 655360 | tf_op jit(solution)/shard_map/all_gather | solution.py:58
  49.9 1.9 %all-to-all-done = bf16[16,8,512]{2,1,0:T(8,128)(2,1)S(1)} async-done(((bf16[16,8,512]{2,1,0:T(8,128)(2,1)}), bf16[16,8,512]{2,1,0:T(8,128)(2,1)S(1)}, u32[]{:S(2)}, u32[]{:S(2)}) %all-to-all-start) | async-done | bytes 131104 | tf_op jit(solution)/shard_map/all_to_all | solution.py:23
  51.7 0.8 %broadcast_in_dim.15 = bf16[4,128,512]{2,1,0:T(8,128)(2,1)} broadcast(bf16[128,512]{1,0:T(8,128)(2,1)S(1)} %bitcast.20), dimensions={1,2} | broadcast | bytes 655360 | tf_op jit(solution)/shard_map/broadcast_in_dim | solution.py:27
  52.6 3.5 %all-to-all-start.1 = ((bf16[4,128,512]{2,1,0:T(8,128)(2,1)}), bf16[4,128,512]{2,1,0:T(8,128)(2,1)S(1)}, u32[]{:S(2)}, u32[]{:S(2)}) async-start(bf16[4,128,512]{2,1,0:T(8,128)(2,1)} %broadcast_in_dim.15), calls=%async_computation.1 | async-start | bytes 1048576 | tf_op jit(solution)/shard_map/all_to_all | solution.py:31
  56.1 1.9 %collective-permute-start = (bf16[256,1024]{1,0:T(8,128)(2,1)S(1)}, bf16[256,1024]{1,0:T(8,128)(2,1)}, u32[]{:S(2)}, u32[]{:S(2)}) collective-permute-start(bf16[256,1024]{1,0:T(8,128)(2,1)S(1)} %bitcast.17), channel_id=1, source_target_pairs={{0,64},{64,0},{1,65},{65,1},{2,66},{66,2},{3,67},{67,3},{4,68},{68... | collective-permute-start | bytes 1572872 | tf_op jit(solution)/shard_map/ppermute | solution.py:61
  58.0 0.0 copy-done.3
  58.0 0.2 copy.8
  58.3 0.0 copy-start.2
  58.3 0.8 %copy-done.2 = bf16[2,512,4,2,32]{1,4,3,2,0:T(8,128)(2,1)} copy-done((bf16[2,512,4,2,32]{1,4,3,2,0:T(8,128)(2,1)}, bf16[2,512,4,2,32]{1,4,3,2,0:T(8,128)(2,1)S(1)}, u32[]{:S(2)}) %copy-start.2) | copy-done | bytes 524312
  59.1 0.5 fusion.1
  59.5 0.0 copy-start
  59.5 0.0 copy-start.1
  59.6 0.4 collective-permute-done
  60.0 1.6 %add_convert_fusion.upper_ref = bf16[512,1024]{1,0:T(8,128)(2,1)S(1)} fusion(f32[512,1024]{1,0:T(8,128)S(1)} %fusion.1, bf16[256,1024]{1,0:T(8,128)(2,1)} %collective-permute-done, bf16[2,512,256]{1,2,0:T(8,128)(2,1)} %bitcast.16, s32[]{:T(128)S(6)} %select_n.8), kind=kOutput, calls=%fused_computation | convolution fusion | flops 269484032 | bytes 3932164 | tf_op jit(solution)/shard_map/dot_general | solution.py:68
  61.6 1.0 %all-to-all-done.1.parts_ref = bf16[4,128,512]{2,1,0:T(8,128)(2,1)S(1)} async-done(((bf16[4,128,512]{2,1,0:T(8,128)(2,1)}), bf16[4,128,512]{2,1,0:T(8,128)(2,1)S(1)}, u32[]{:S(2)}, u32[]{:S(2)}) %all-to-all-start.1) | async-done | bytes 524320 | tf_op jit(solution)/shard_map/all_to_all | solution.py:31
  62.6 0.0 copy-done
  62.6 0.0 copy-done.1
  62.6 1.7 %update.1 = bf16[512,1024]{1,0:T(8,128)(2,1)} custom-call(bf16[4,128,512]{2,1,0:T(8,128)(2,1)S(1)} %all-to-all-done.1.parts_ref, bf16[512,512]{1,0:T(8,128)(2,1)S(1)} %copy-done.1, bf16[512,1024]{1,0:T(8,128)(2,1)S(1)} %add_convert_fusion.upper_ref, bf16[512,1024]{1,0:T(8,128)(2,1)S(1)} %copy-done), custom_call_target="tpu_custom_call" | custom-call | flops 805306368 | bytes 4194304 | tf_op jit(solution)/shard_map/update/pallas_call | solution.py:71
  (1 shorter events, 0.0 us)
Async XLA Ops:
  0.0 58.0 %copy-start.3 = (bf16[512,512]{1,0:T(8,128)(2,1)S(1)}, bf16[512,512]{1,0:T(8,128)(2,1)}, u32[]{:S(2)}) copy-start(bf16[512,512]{1,0:T(8,128)(2,1)} %param.8) | copy-start | bytes 1572868
  1.4 50.3 %all-to-all-start = ((bf16[16,8,512]{2,1,0:T(8,128)(2,1)}), bf16[16,8,512]{2,1,0:T(8,128)(2,1)S(1)}, u32[]{:S(2)}, u32[]{:S(2)}) async-start(bf16[16,8,512]{2,1,0:T(8,128)(2,1)} %broadcast_in_dim.6), calls=%async_computation | async-start | bytes 262144 | tf_op jit(solution)/shard_map/all_to_all | solution.py:23
  52.6 10.0 %all-to-all-start.1 = ((bf16[4,128,512]{2,1,0:T(8,128)(2,1)}), bf16[4,128,512]{2,1,0:T(8,128)(2,1)S(1)}, u32[]{:S(2)}, u32[]{:S(2)}) async-start(bf16[4,128,512]{2,1,0:T(8,128)(2,1)} %broadcast_in_dim.15), calls=%async_computation.1 | async-start | bytes 1048576 | tf_op jit(solution)/shard_map/all_to_all | solution.py:31
  56.1 3.9 %collective-permute-start = (bf16[256,1024]{1,0:T(8,128)(2,1)S(1)}, bf16[256,1024]{1,0:T(8,128)(2,1)}, u32[]{:S(2)}, u32[]{:S(2)}) collective-permute-start(bf16[256,1024]{1,0:T(8,128)(2,1)S(1)} %bitcast.17), channel_id=1, source_target_pairs={{0,64},{64,0},{1,65},{65,1},{2,66},{66,2},{3,67},{67,3},{4,68},{68... | collective-permute-start | bytes 1572872 | tf_op jit(solution)/shard_map/ppermute | solution.py:61
  58.3 0.8 %copy-start.2 = (bf16[2,512,4,2,32]{1,4,3,2,0:T(8,128)(2,1)}, bf16[2,512,4,2,32]{1,4,3,2,0:T(8,128)(2,1)S(1)}, u32[]{:S(2)}) copy-start(bf16[2,512,4,2,32]{1,4,3,2,0:T(8,128)(2,1)S(1)} %copy.9) | copy-start | bytes 1572868
  59.5 3.1 %copy-start = (bf16[512,1024]{1,0:T(8,128)(2,1)S(1)}, bf16[512,1024]{1,0:T(8,128)(2,1)}, u32[]{:S(2)}) copy-start(bf16[512,1024]{1,0:T(8,128)(2,1)} %trailing_ref.1) | copy-start | bytes 3145732
  59.5 3.1 %copy-start.1 = (bf16[512,512]{1,0:T(8,128)(2,1)S(1)}, bf16[512,512]{1,0:T(8,128)(2,1)}, u32[]{:S(2)}) copy-start(bf16[512,512]{1,0:T(8,128)(2,1)} %inverse_ref.1) | copy-start | bytes 1572868

commit v3 on v2

--- a/solution.py
+++ b/solution.py
@@ -11,7 +11,7 @@
 SIZES = (2, 4, 2, 2, 32)
 NEAR = 2
 FAR = 32 // NEAR
-FIRST = 24
+FIRST = 22
 ORDER = [(FIRST + NEAR * i) % 32 // NEAR for i in range(FAR)]
 GROUPS = [[NEAR * i + j for i in ORDER] for j in range(NEAR)]
 SWAP = [(0, 1), (1, 0)]

time: 64.9 us -> 63.6 us (0.980)
  waiting for transfers between devices: 3.29 us -> 1.43 us
    all_to_all x1, waiting for transfers between devices: 1.86 us -> 0.01 us  [gather_far(): return lax.all_to_all(copies, 'z', 0, 0, axis_index_groups=GROUPS)]
  transfers between devices with their start and end apart: 3 -> 3, of which waited for: 3 -> 2; matrix products, arithmetic and copies ran while one was open for 4% -> 4% of each run, Pallas kernels for 0% -> 0%
where the time goes in v3:
time: 63.6 us; the launch traced here: 62.5 us
  starting transfers between devices  34.3 us (54%)
  blocking collectives  19.5 us (31%)
  local copies, waits for them, and re-layouts  3.31 us (5%)
  matrix products  2.07 us (3%)
  Pallas kernels  1.74 us (3%)
  waiting for transfers between devices  1.43 us (2%)
    all_to_all x1, starting transfers between devices, gather_far(): return lax.all_to_all(copies, 'z', 0, 0, axis_index_groups=GROUPS)  28.9 us
    all_gather x1, blocking collectives, on_device(): upper = lax.all_gather(upper, 'x', axis=0).reshape(256, 1024)  12.9 us
    all_gather x1, blocking collectives, on_device(): upper = lax.all_gather(upper_raw, 'y_hi', axis=0)  6.65 us
    all_to_all x1, starting transfers between devices, gather_near(): return lax.all_to_all(copies, ('y_lo', 'z'), 0, 0, axis_index_groups=groups)  3.47 us
    ppermute x1, starting transfers between devices, on_device(): other = lax.ppermute(upper, 'core', SWAP)  1.92 us
    pallas_call x1, Pallas kernels, on_device(): pl.pallas_call(update, out_shape=jax.ShapeDtypeStruct((512, 1024), jnp.bf...  1.74 us
    dot_general x1, matrix products, on_device(): jnp.dot(theirs, other, preferred_element_type=jnp.float32)  1.61 us
    broadcast_in_dim x1, local copies, waits for them, and re-layouts, gather_far(): copies = jnp.broadcast_to(block[None], (FAR,) + block.shape)  1.42 us
  transfers between devices with their start and end apart: 3, of which 2 were waited for; matrix products, arithmetic and copies ran while one was open for 4% of the time, Pallas kernels for 0%

profile of v3, /device:TPU:6, one launch (start us, length us, event | category | flops | bytes accessed | tf_op | source)
XLA Modules:
  0.0 62.5 jit_solution(3170517161420733113)
XLA Ops:
  0.0 0.0 copy-start.3
  0.0 1.4 %broadcast_in_dim.6 = bf16[16,8,512]{2,1,0:T(8,128)(2,1)} broadcast(bf16[8,512]{1,0:T(8,128)(2,1)} %param.6), dimensions={1,2} | broadcast | bytes 139264 | tf_op jit(solution)/shard_map/broadcast_in_dim | solution.py:22
  1.4 28.9 %all-to-all-start = ((bf16[16,8,512]{2,1,0:T(8,128)(2,1)}), bf16[16,8,512]{2,1,0:T(8,128)(2,1)S(1)}, u32[]{:S(2)}, u32[]{:S(2)}) async-start(bf16[16,8,512]{2,1,0:T(8,128)(2,1)} %broadcast_in_dim.6), calls=%async_computation | async-start | bytes 262144 | tf_op jit(solution)/shard_map/all_to_all | solution.py:23
  30.3 6.6 %all-gather = bf16[64,1024]{1,0:T(8,128)(2,1)S(1)} all-gather(bf16[32,1024]{1,0:T(8,128)(2,1)} %param.7), channel_id=2, replica_groups=mesh['y_hi'=2,'x'=4,'core'=2,'y_lo'=2,'z'=32] {'y_hi'}, dimensions={0}, use_global_device_ids=true | all-gather | bytes 196608 | tf_op jit(solution)/shard_map/all_gather | solution.py:57
  37.0 12.9 %all-gather.1 = bf16[8,32,1024]{2,1,0:T(8,128)(2,1)S(1)} all-gather(bf16[2,32,1024]{2,1,0:T(8,128)(2,1)S(1)} %bitcast.21), channel_id=3, replica_groups=mesh['y_hi'=2,'x'=4,'core'=2,'y_lo'=2,'z'=32] {'x'}, dimensions={0}, use_global_device_ids=true | all-gather | bytes 655360 | tf_op jit(solution)/shard_map/all_gather | solution.py:58
  49.9 0.0 all-to-all-done
  49.9 0.8 %broadcast_in_dim.15 = bf16[4,128,512]{2,1,0:T(8,128)(2,1)} broadcast(bf16[128,512]{1,0:T(8,128)(2,1)S(1)} %bitcast.20), dimensions={1,2} | broadcast | bytes 655360 | tf_op jit(solution)/shard_map/broadcast_in_dim | solution.py:27
  50.7 3.5 %all-to-all-start.1 = ((bf16[4,128,512]{2,1,0:T(8,128)(2,1)}), bf16[4,128,512]{2,1,0:T(8,128)(2,1)S(1)}, u32[]{:S(2)}, u32[]{:S(2)}) async-start(bf16[4,128,512]{2,1,0:T(8,128)(2,1)} %broadcast_in_dim.15), calls=%async_computation.1 | async-start | bytes 1048576 | tf_op jit(solution)/shard_map/all_to_all | solution.py:31
  54.2 1.9 %collective-permute-start = (bf16[256,1024]{1,0:T(8,128)(2,1)S(1)}, bf16[256,1024]{1,0:T(8,128)(2,1)}, u32[]{:S(2)}, u32[]{:S(2)}) collective-permute-start(bf16[256,1024]{1,0:T(8,128)(2,1)S(1)} %bitcast.17), channel_id=1, source_target_pairs={{0,64},{64,0},{1,65},{65,1},{2,66},{66,2},{3,67},{67,3},{4,68},{68... | collective-permute-start | bytes 1572872 | tf_op jit(solution)/shard_map/ppermute | solution.py:61
  56.1 0.0 copy-done.3
  56.1 0.2 copy.8
  56.4 0.0 copy-start.2
  56.4 0.8 %copy-done.2 = bf16[2,512,4,2,32]{1,4,3,2,0:T(8,128)(2,1)} copy-done((bf16[2,512,4,2,32]{1,4,3,2,0:T(8,128)(2,1)}, bf16[2,512,4,2,32]{1,4,3,2,0:T(8,128)(2,1)S(1)}, u32[]{:S(2)}) %copy-start.2) | copy-done | bytes 524312
  57.2 0.5 fusion.1
  57.7 0.0 copy-start
  57.7 0.0 copy-start.1
  57.7 0.4 collective-permute-done
  58.1 1.6 %add_convert_fusion.upper_ref = bf16[512,1024]{1,0:T(8,128)(2,1)S(1)} fusion(f32[512,1024]{1,0:T(8,128)S(1)} %fusion.1, bf16[256,1024]{1,0:T(8,128)(2,1)} %collective-permute-done, bf16[2,512,256]{1,2,0:T(8,128)(2,1)} %bitcast.16, s32[]{:T(128)S(6)} %select_n.8), kind=kOutput, calls=%fused_computation | convolution fusion | flops 269484032 | bytes 3932164 | tf_op jit(solution)/shard_map/dot_general | solution.py:68
  59.7 1.0 %all-to-all-done.1.parts_ref = bf16[4,128,512]{2,1,0:T(8,128)(2,1)S(1)} async-done(((bf16[4,128,512]{2,1,0:T(8,128)(2,1)}), bf16[4,128,512]{2,1,0:T(8,128)(2,1)S(1)}, u32[]{:S(2)}, u32[]{:S(2)}) %all-to-all-start.1) | async-done | bytes 524320 | tf_op jit(solution)/shard_map/all_to_all | solution.py:31
  60.7 0.0 copy-done
  60.7 0.0 copy-done.1
  60.7 1.7 %update.1 = bf16[512,1024]{1,0:T(8,128)(2,1)} custom-call(bf16[4,128,512]{2,1,0:T(8,128)(2,1)S(1)} %all-to-all-done.1.parts_ref, bf16[512,512]{1,0:T(8,128)(2,1)S(1)} %copy-done.1, bf16[512,1024]{1,0:T(8,128)(2,1)S(1)} %add_convert_fusion.upper_ref, bf16[512,1024]{1,0:T(8,128)(2,1)S(1)} %copy-done), custom_call_target="tpu_custom_call" | custom-call | flops 805306368 | bytes 4194304 | tf_op jit(solution)/shard_map/update/pallas_call | solution.py:71
  (1 shorter events, 0.0 us)
Async XLA Ops:
  0.0 56.1 %copy-start.3 = (bf16[512,512]{1,0:T(8,128)(2,1)S(1)}, bf16[512,512]{1,0:T(8,128)(2,1)}, u32[]{:S(2)}) copy-start(bf16[512,512]{1,0:T(8,128)(2,1)} %param.8) | copy-start | bytes 1572868
  1.4 48.5 %all-to-all-start = ((bf16[16,8,512]{2,1,0:T(8,128)(2,1)}), bf16[16,8,512]{2,1,0:T(8,128)(2,1)S(1)}, u32[]{:S(2)}, u32[]{:S(2)}) async-start(bf16[16,8,512]{2,1,0:T(8,128)(2,1)} %broadcast_in_dim.6), calls=%async_computation | async-start | bytes 262144 | tf_op jit(solution)/shard_map/all_to_all | solution.py:23
  50.7 10.0 %all-to-all-start.1 = ((bf16[4,128,512]{2,1,0:T(8,128)(2,1)}), bf16[4,128,512]{2,1,0:T(8,128)(2,1)S(1)}, u32[]{:S(2)}, u32[]{:S(2)}) async-start(bf16[4,128,512]{2,1,0:T(8,128)(2,1)} %broadcast_in_dim.15), calls=%async_computation.1 | async-start | bytes 1048576 | tf_op jit(solution)/shard_map/all_to_all | solution.py:31
  54.2 3.9 %collective-permute-start = (bf16[256,1024]{1,0:T(8,128)(2,1)S(1)}, bf16[256,1024]{1,0:T(8,128)(2,1)}, u32[]{:S(2)}, u32[]{:S(2)}) collective-permute-start(bf16[256,1024]{1,0:T(8,128)(2,1)S(1)} %bitcast.17), channel_id=1, source_target_pairs={{0,64},{64,0},{1,65},{65,1},{2,66},{66,2},{3,67},{67,3},{4,68},{68... | collective-permute-start | bytes 1572872 | tf_op jit(solution)/shard_map/ppermute | solution.py:61
  56.4 0.8 %copy-start.2 = (bf16[2,512,4,2,32]{1,4,3,2,0:T(8,128)(2,1)}, bf16[2,512,4,2,32]{1,4,3,2,0:T(8,128)(2,1)S(1)}, u32[]{:S(2)}) copy-start(bf16[2,512,4,2,32]{1,4,3,2,0:T(8,128)(2,1)S(1)} %copy.9) | copy-start | bytes 1572868
  57.7 3.1 %copy-start = (bf16[512,1024]{1,0:T(8,128)(2,1)S(1)}, bf16[512,1024]{1,0:T(8,128)(2,1)}, u32[]{:S(2)}) copy-start(bf16[512,1024]{1,0:T(8,128)(2,1)} %trailing_ref.1) | copy-start | bytes 3145732
  57.7 3.1 %copy-start.1 = (bf16[512,512]{1,0:T(8,128)(2,1)S(1)}, bf16[512,512]{1,0:T(8,128)(2,1)}, u32[]{:S(2)}) copy-start(bf16[512,512]{1,0:T(8,128)(2,1)} %inverse_ref.1) | copy-start | bytes 1572868

commit v4 on v3

--- a/solution.py
+++ b/solution.py
@@ -1,5 +1,3 @@
-import functools
-
 import jax
 import jax.numpy as jnp
 from jax import lax
@@ -52,10 +50,9 @@
 
 def on_device(trailing, lower_raw, upper_raw, lower_inv, upper_inv):
     core = lax.axis_index("core")
-    y_hi = lax.axis_index("y_hi")
     far = gather_far(lower_raw)
-    upper = lax.all_gather(upper_raw, "y_hi", axis=0)
-    upper = lax.all_gather(upper, "x", axis=0).reshape(256, 1024)
+    upper = lax.all_gather(upper_raw, "y_hi", axis=0, tiled=True)
+    upper = lax.all_gather(upper, "x", axis=0, tiled=True)
     far, upper = lax.optimization_barrier((far, upper))
     parts = gather_near(far.reshape(ROWS, 512))
     other = lax.ppermute(upper, "core", SWAP)

time: 63.6 us -> 63.6 us (level)
  no operation moved by 1% of the time
where the time goes in v4:
time: 63.6 us; the launch traced here: 62.5 us
  starting transfers between devices  34.3 us (54%)
  blocking collectives  19.5 us (31%)
  local copies, waits for them, and re-layouts  3.31 us (5%)
  matrix products  2.07 us (3%)
  Pallas kernels  1.74 us (3%)
  waiting for transfers between devices  1.43 us (2%)
    all_to_all x1, starting transfers between devices, gather_far(): return lax.all_to_all(copies, 'z', 0, 0, axis_index_groups=GROUPS)  28.9 us
    all_gather x1, blocking collectives, on_device(): upper = lax.all_gather(upper, 'x', axis=0, tiled=True)  12.9 us
    all_gather x1, blocking collectives, on_device(): upper = lax.all_gather(upper_raw, 'y_hi', axis=0, tiled=True)  6.65 us
    all_to_all x1, starting transfers between devices, gather_near(): return lax.all_to_all(copies, ('y_lo', 'z'), 0, 0, axis_index_groups=groups)  3.47 us
    ppermute x1, starting transfers between devices, on_device(): other = lax.ppermute(upper, 'core', SWAP)  1.92 us
    pallas_call x1, Pallas kernels, on_device(): pl.pallas_call(update, out_shape=jax.ShapeDtypeStruct((512, 1024), jnp.bf...  1.74 us
    dot_general x1, matrix products, on_device(): jnp.dot(theirs, other, preferred_element_type=jnp.float32)  1.61 us
    broadcast_in_dim x1, local copies, waits for them, and re-layouts, gather_far(): copies = jnp.broadcast_to(block[None], (FAR,) + block.shape)  1.42 us
  transfers between devices with their start and end apart: 3, of which 2 were waited for; matrix products, arithmetic and copies ran while one was open for 4% of the time, Pallas kernels for 0%

profile of v4, /device:TPU:6, one launch (start us, length us, event | category | flops | bytes accessed | tf_op | source)
XLA Modules:
  0.0 62.5 jit_solution(10580529680673901304)
XLA Ops:
  0.0 0.0 copy-start.3
  0.0 1.4 %broadcast_in_dim.6 = bf16[16,8,512]{2,1,0:T(8,128)(2,1)} broadcast(bf16[8,512]{1,0:T(8,128)(2,1)} %param.6), dimensions={1,2} | broadcast | bytes 139264 | tf_op jit(solution)/shard_map/broadcast_in_dim | solution.py:20
  1.4 28.9 %all-to-all-start = ((bf16[16,8,512]{2,1,0:T(8,128)(2,1)}), bf16[16,8,512]{2,1,0:T(8,128)(2,1)S(1)}, u32[]{:S(2)}, u32[]{:S(2)}) async-start(bf16[16,8,512]{2,1,0:T(8,128)(2,1)} %broadcast_in_dim.6), calls=%async_computation | async-start | bytes 262144 | tf_op jit(solution)/shard_map/all_to_all | solution.py:21
  30.3 6.6 %all_gather.6 = bf16[64,1024]{1,0:T(8,128)(2,1)S(1)} all-gather(bf16[32,1024]{1,0:T(8,128)(2,1)} %param.7), channel_id=1, replica_groups=mesh['y_hi'=2,'x'=4,'core'=2,'y_lo'=2,'z'=32] {'y_hi'}, dimensions={0}, use_global_device_ids=true | all-gather | bytes 196608 | tf_op jit(solution)/shard_map/all_gather | solution.py:54
  37.0 12.9 %all_gather.7 = bf16[256,1024]{1,0:T(8,128)(2,1)S(1)} all-gather(bf16[64,1024]{1,0:T(8,128)(2,1)S(1)} %all_gather.6), channel_id=1, replica_groups=mesh['y_hi'=2,'x'=4,'core'=2,'y_lo'=2,'z'=32] {'x'}, dimensions={0}, use_global_device_ids=true | all-gather | bytes 655360 | tf_op jit(solution)/shard_map/all_gather | solution.py:55
  49.9 0.0 all-to-all-done
  49.9 0.8 %broadcast_in_dim.15 = bf16[4,128,512]{2,1,0:T(8,128)(2,1)} broadcast(bf16[128,512]{1,0:T(8,128)(2,1)S(1)} %bitcast.16), dimensions={1,2} | broadcast | bytes 655360 | tf_op jit(solution)/shard_map/broadcast_in_dim | solution.py:25
  50.7 3.5 %all-to-all-start.1 = ((bf16[4,128,512]{2,1,0:T(8,128)(2,1)}), bf16[4,128,512]{2,1,0:T(8,128)(2,1)S(1)}, u32[]{:S(2)}, u32[]{:S(2)}) async-start(bf16[4,128,512]{2,1,0:T(8,128)(2,1)} %broadcast_in_dim.15), calls=%async_computation.1 | async-start | bytes 1048576 | tf_op jit(solution)/shard_map/all_to_all | solution.py:29
  54.2 1.9 %collective-permute-start = (bf16[256,1024]{1,0:T(8,128)(2,1)S(1)}, bf16[256,1024]{1,0:T(8,128)(2,1)}, u32[]{:S(2)}, u32[]{:S(2)}) collective-permute-start(bf16[256,1024]{1,0:T(8,128)(2,1)S(1)} %all_gather.7), channel_id=1, source_target_pairs={{0,64},{64,0},{1,65},{65,1},{2,66},{66,2},{3,67},{67,3},{4,68},{68... | collective-permute-start | bytes 1572872 | tf_op jit(solution)/shard_map/ppermute | solution.py:58
  56.1 0.0 copy-done.3
  56.1 0.2 copy.6
  56.4 0.0 copy-start.2
  56.4 0.8 %copy-done.2 = bf16[2,512,4,2,32]{1,4,3,2,0:T(8,128)(2,1)} copy-done((bf16[2,512,4,2,32]{1,4,3,2,0:T(8,128)(2,1)}, bf16[2,512,4,2,32]{1,4,3,2,0:T(8,128)(2,1)S(1)}, u32[]{:S(2)}) %copy-start.2) | copy-done | bytes 524312
  57.2 0.5 fusion.1
  57.7 0.0 copy-start
  57.7 0.0 copy-start.1
  57.7 0.4 collective-permute-done
  58.1 1.6 %add_convert_fusion.upper_ref = bf16[512,1024]{1,0:T(8,128)(2,1)S(1)} fusion(f32[512,1024]{1,0:T(8,128)S(1)} %fusion.1, bf16[256,1024]{1,0:T(8,128)(2,1)} %collective-permute-done, bf16[2,512,256]{1,2,0:T(8,128)(2,1)} %bitcast.14, s32[]{:T(128)S(6)} %select_n.8), kind=kOutput, calls=%fused_computation | convolution fusion | flops 269484032 | bytes 3932164 | tf_op jit(solution)/shard_map/dot_general | solution.py:65
  59.7 1.0 %all-to-all-done.1.parts_ref = bf16[4,128,512]{2,1,0:T(8,128)(2,1)S(1)} async-done(((bf16[4,128,512]{2,1,0:T(8,128)(2,1)}), bf16[4,128,512]{2,1,0:T(8,128)(2,1)S(1)}, u32[]{:S(2)}, u32[]{:S(2)}) %all-to-all-start.1) | async-done | bytes 524320 | tf_op jit(solution)/shard_map/all_to_all | solution.py:29
  60.7 0.0 copy-done
  60.7 0.0 copy-done.1
  60.7 1.7 %update.1 = bf16[512,1024]{1,0:T(8,128)(2,1)} custom-call(bf16[4,128,512]{2,1,0:T(8,128)(2,1)S(1)} %all-to-all-done.1.parts_ref, bf16[512,512]{1,0:T(8,128)(2,1)S(1)} %copy-done.1, bf16[512,1024]{1,0:T(8,128)(2,1)S(1)} %add_convert_fusion.upper_ref, bf16[512,1024]{1,0:T(8,128)(2,1)S(1)} %copy-done), custom_call_target="tpu_custom_call" | custom-call | flops 805306368 | bytes 4194304 | tf_op jit(solution)/shard_map/update/pallas_call | solution.py:68
  (1 shorter events, 0.0 us)
Async XLA Ops:
  0.0 56.1 %copy-start.3 = (bf16[512,512]{1,0:T(8,128)(2,1)S(1)}, bf16[512,512]{1,0:T(8,128)(2,1)}, u32[]{:S(2)}) copy-start(bf16[512,512]{1,0:T(8,128)(2,1)} %param.8) | copy-start | bytes 1572868
  1.4 48.5 %all-to-all-start = ((bf16[16,8,512]{2,1,0:T(8,128)(2,1)}), bf16[16,8,512]{2,1,0:T(8,128)(2,1)S(1)}, u32[]{:S(2)}, u32[]{:S(2)}) async-start(bf16[16,8,512]{2,1,0:T(8,128)(2,1)} %broadcast_in_dim.6), calls=%async_computation | async-start | bytes 262144 | tf_op jit(solution)/shard_map/all_to_all | solution.py:21
  50.7 10.0 %all-to-all-start.1 = ((bf16[4,128,512]{2,1,0:T(8,128)(2,1)}), bf16[4,128,512]{2,1,0:T(8,128)(2,1)S(1)}, u32[]{:S(2)}, u32[]{:S(2)}) async-start(bf16[4,128,512]{2,1,0:T(8,128)(2,1)} %broadcast_in_dim.15), calls=%async_computation.1 | async-start | bytes 1048576 | tf_op jit(solution)/shard_map/all_to_all | solution.py:29
  54.2 3.9 %collective-permute-start = (bf16[256,1024]{1,0:T(8,128)(2,1)S(1)}, bf16[256,1024]{1,0:T(8,128)(2,1)}, u32[]{:S(2)}, u32[]{:S(2)}) collective-permute-start(bf16[256,1024]{1,0:T(8,128)(2,1)S(1)} %all_gather.7), channel_id=1, source_target_pairs={{0,64},{64,0},{1,65},{65,1},{2,66},{66,2},{3,67},{67,3},{4,68},{68... | collective-permute-start | bytes 1572872 | tf_op jit(solution)/shard_map/ppermute | solution.py:58
  56.4 0.8 %copy-start.2 = (bf16[2,512,4,2,32]{1,4,3,2,0:T(8,128)(2,1)}, bf16[2,512,4,2,32]{1,4,3,2,0:T(8,128)(2,1)S(1)}, u32[]{:S(2)}) copy-start(bf16[2,512,4,2,32]{1,4,3,2,0:T(8,128)(2,1)S(1)} %copy.7) | copy-start | bytes 1572868
  57.7 3.1 %copy-start = (bf16[512,1024]{1,0:T(8,128)(2,1)S(1)}, bf16[512,1024]{1,0:T(8,128)(2,1)}, u32[]{:S(2)}) copy-start(bf16[512,1024]{1,0:T(8,128)(2,1)} %trailing_ref.1) | copy-start | bytes 3145732
  57.7 3.1 %copy-start.1 = (bf16[512,512]{1,0:T(8,128)(2,1)S(1)}, bf16[512,512]{1,0:T(8,128)(2,1)}, u32[]{:S(2)}) copy-start(bf16[512,512]{1,0:T(8,128)(2,1)} %inverse_ref.1) | copy-start | bytes 1572868
